TPU v7x, 256 devices: a whole 4x4x8 slice. The times are simulated.
256 devices in a mesh: leaf: 64 (over x, z, core), blk: 4 (over y).
Axes of the slice: x: 4, y: 4, z: 8, core: 2. Of those that a mesh axis runs over, the one named last changes fastest.
Arguments:
- sources: bfloat16 [128, 1048576], P(None, ('leaf', 'blk')), may hold values from -6 to 6
- near_blocks: bfloat16 [8192, 6, 128, 128], P(('leaf', 'blk')), may hold values from -0.21875 to 0.21875
- near_cols: int32 [8192, 6], P(('leaf', 'blk')), may hold values from 0 to 8191, as said below
- basis: bfloat16 [8192, 64, 128], P(('leaf', 'blk')), may hold values from -0.046875 to 0.046875
- transfer: bfloat16 [126, 64, 64], replicated, may hold values from -0.75 to 0.75
- coupling: bfloat16 [126, 64, 64], replicated, may hold values from -0.75 to 0.75
Outputs:
- potential: float32 [128, 1048576], P(None, ('leaf', 'blk'))
Inputs may be any that keep to these rules, and one draw needn't show every extreme that they name: `near_cols`: for cluster c the entries are c, min(c + 4, 8191), max(c - 4, 0), then entries within 4 clusters of c, clipped to the grid of clusters.
All inputs are finite; a program needn't handle non-finite values.
Results may differ from a plain program's by a relative error of at most 0.0012.
Values may be sent and summed in bfloat16 or wider, within the bound.
No kernel may reach another device: no remote copies, remote signals or barrier semaphores. Data moves between devices by JAX's collectives and lax.ppermute only.
A program may use at most 128 MiB of HBM per device.

v0:
```python
import jax
import jax.numpy as jnp
from jax import lax
from jax.sharding import PartitionSpec as P

REACH = 4
highest = lax.Precision.HIGHEST


def padded(cells, sides, width):
    for axis, dim in sides:
        count = lax.axis_size(axis)
        ends = count - 1
        head = lax.slice_in_dim(cells, 0, width, axis=dim)
        tail = lax.slice_in_dim(cells, cells.shape[dim] - width, cells.shape[dim], axis=dim)
        cells = jnp.concatenate(
            [
                lax.ppermute(tail, axis, [(i, (i + 1) % count) for i in range(ends)]),
                cells,
                lax.ppermute(head, axis, [((i + 1) % count, i) for i in range(ends)]),
            ],
            axis=dim,
        )
    return cells


def from_partner(value, axis, distance):
    mask = 2**distance
    pairs = [(source, source ^ mask) for source in range(lax.axis_size(axis))]
    return lax.ppermute(value, axis, pairs)


def pick_matrix(table, table_row):
    return lax.dynamic_index_in_dim(table, table_row, 0, keepdims=False).astype(jnp.float32)


def body(sources, near_blocks, near_cols, basis, transfer, coupling):
    rhs_count = sources.shape[0]
    own_clusters = near_blocks.shape[0]
    near_count = near_blocks.shape[1]
    panel_size = near_blocks.shape[2]
    leaf_count = lax.axis_size("leaf")
    levels = leaf_count.bit_length() - 1
    leaf_index = lax.axis_index("leaf")
    extended = padded(sources, ((("leaf", "blk"), 1),), REACH * panel_size)
    by_cluster = jnp.transpose(
        extended.reshape(rhs_count, own_clusters + 2 * REACH, panel_size), (1, 0, 2)
    )
    own_sources = by_cluster[REACH : REACH + own_clusters]
    partial_value = jnp.einsum(
        "crp,ckp->rk", own_sources, basis, preferred_element_type=jnp.float32
    )
    moment = lax.psum(partial_value, "blk")
    first_cluster = lax.axis_index(("leaf", "blk")) * own_clusters
    local_columns = near_cols - (first_cluster - REACH)
    near = jnp.zeros((own_clusters, rhs_count, panel_size), jnp.float32)
    for slot in range(near_count):
        picked = jnp.take(by_cluster, local_columns[:, slot], axis=0)
        near = near + jnp.einsum(
            "crp,cpq->crq", picked, near_blocks[:, slot], preferred_element_type=jnp.float32
        )
    siblings = []
    current = moment
    for level in range(levels):
        sibling_moment = from_partner(current, "leaf", level)
        siblings.append(sibling_moment)
        if level + 1 < levels:
            node_count = leaf_count >> level
            node_index = leaf_index >> level
            mine = pick_matrix(transfer, node_count - 2 + node_index)
            theirs = pick_matrix(transfer, node_count - 2 + (node_index ^ 1))
            current = jnp.dot(current, mine, precision=highest) + jnp.dot(
                sibling_moment, theirs, precision=highest
            )
    local_terms = []
    for level in range(levels):
        node_count = leaf_count >> level
        couple = pick_matrix(coupling, node_count - 2 + (leaf_index >> level))
        local_terms.append(jnp.dot(siblings[level], couple, precision=highest))
    descended = local_terms[levels - 1]
    for level in range(levels - 2, -1, -1):
        node_count = leaf_count >> level
        up_matrix = pick_matrix(transfer, node_count - 2 + (leaf_index >> level))
        descended = local_terms[level] + jnp.dot(descended, up_matrix.T, precision=highest)
    leaf_local = descended.astype(jnp.bfloat16)
    far = jnp.einsum("rk,ckp->crp", leaf_local, basis, preferred_element_type=jnp.float32)
    total = near + far
    return jnp.transpose(total, (1, 0, 2)).reshape(rhs_count, own_clusters * panel_size)


def solution(mesh):
    return jax.shard_map(
        body,
        mesh=mesh,
        in_specs=(
            P(None, ("leaf", "blk")),
            P(("leaf", "blk"), None, None, None),
            P(("leaf", "blk"), None),
            P(("leaf", "blk"), None, None),
            P(),
            P(),
        ),
        out_specs=P(None, ("leaf", "blk")),
        check_vma=False,
    )
```

profile of v0, /device:TPU:2, one launch (start us, length us, event | category | flops | bytes accessed | tf_op | source)
XLA Modules:
  0.0 128.4 jit_solution(17000539796109426428)
XLA Ops:
  0.0 1.7 %copy.14 = bf16[128,4096]{0,1:T(8,128)(2,1)S(1)} copy(bf16[128,4096]{1,0:T(8,128)(2,1)} %param.8) | data formatting | bytes 2097152 | tf_op args[0]
  1.8 3.5 %collective-permute-start = (bf16[128,512]{0,1:T(8,128)(2,1)S(1)}, bf16[128,512]{0,1:T(8,128)(2,1)S(1)}, u32[]{:S(2)}, u32[]{:S(2)}) collective-permute-start(bf16[128,512]{0,1:T(8,128)(2,1)S(1)} %get-tuple-element.34), channel_id=1, source_target_pairs={{0,1},{1,2},{2,3},{3,4},{4,5},{5,6},{6,7},{7,8},{8,9},{9,10},{10,1... | collective-permute-start | bytes 393224 | tf_op jit(solution)/shard_map/ppermute | solution.py:18
  5.3 8.1 %collective-permute-start.1 = (bf16[128,512]{0,1:T(8,128)(2,1)S(1)}, bf16[128,512]{0,1:T(8,128)(2,1)S(1)}, u32[]{:S(2)}, u32[]{:S(2)}) collective-permute-start(bf16[128,512]{0,1:T(8,128)(2,1)S(1)} %get-tuple-element.35), channel_id=1, source_target_pairs={{1,0},{2,1},{3,2},{4,3},{5,4},{6,5},{7,6},{8,7},{9,8},{10,9},{11,1... | collective-permute-start | bytes 393224 | tf_op jit(solution)/shard_map/ppermute | solution.py:20
  13.5 4.6 %constant_dynamic-slice_fusion.15 = (bf16[1,64,64]{0,2,1:T(8,128)(2,1)}, bf16[1,64,64]{0,2,1:T(8,128)(2,1)}, bf16[1,64,64]{0,2,1:T(8,128)(2,1)}, bf16[1,64,64]{0...) fusion(bf16[126,64,64]{0,2,1:T(8,128)(2,1)S(1)} %copy-done.2, s32[]{:T(128)S(6)} %select_n.51, ...), kind=kLoop, calls=%fused_computation.109 | loop fusion | bytes 98328 | tf_op jit(solution)/shard_map/jit(dynamic_index_in_dim)/dynamic_slice | solution.py:34
  18.1 7.1 %constant_dynamic-slice_fusion.1 = (bf16[1,64,64]{0,2,1:T(8,128)(2,1)S(1)}, bf16[1,64,64]{0,2,1:T(8,128)(2,1)}, bf16[1,64,64]{0,2,1:T(8,128)(2,1)}, bf16[1,64,64...) fusion(bf16[126,64,64]{0,2,1:T(8,128)(2,1)S(1)} %copy-done.1, ...), kind=kLoop, calls=%fused_computation.95 | loop fusion | bytes 163880 | tf_op jit(solution)/shard_map/jit(dynamic_index_in_dim)/dynamic_slice | solution.py:34
  25.3 1.7 %copy.48 = bf16[1,64,64]{2,1,0:T(8,128)(2,1)S(1)} copy(bf16[1,64,64]{0,2,1:T(8,128)(2,1)} %get-tuple-element.33) | data formatting | bytes 16384
  27.0 1.7 %copy.49 = bf16[1,64,64]{2,1,0:T(8,128)(2,1)S(1)} copy(bf16[1,64,64]{0,2,1:T(8,128)(2,1)} %get-tuple-element.32) | data formatting | bytes 16384
  28.6 1.7 %copy.51 = bf16[1,64,64]{2,1,0:T(8,128)(2,1)S(1)} copy(bf16[1,64,64]{0,2,1:T(8,128)(2,1)} %get-tuple-element.31) | data formatting | bytes 16384
  30.3 1.7 %copy.52 = bf16[1,64,64]{2,1,0:T(8,128)(2,1)S(1)} copy(bf16[1,64,64]{0,2,1:T(8,128)(2,1)} %get-tuple-element.30) | data formatting | bytes 16384
  32.0 1.7 %copy.54 = bf16[1,64,64]{2,1,0:T(8,128)(2,1)S(1)} copy(bf16[1,64,64]{0,2,1:T(8,128)(2,1)} %get-tuple-element.29) | data formatting | bytes 16384
  33.7 1.7 %copy.55 = bf16[1,64,64]{2,1,0:T(8,128)(2,1)S(1)} copy(bf16[1,64,64]{0,2,1:T(8,128)(2,1)} %get-tuple-element.28) | data formatting | bytes 16384
  35.4 1.7 %copy.57 = bf16[1,64,64]{2,1,0:T(8,128)(2,1)S(1)} copy(bf16[1,64,64]{0,2,1:T(8,128)(2,1)} %get-tuple-element.27) | data formatting | bytes 16384
  37.1 1.7 %copy.58 = bf16[1,64,64]{2,1,0:T(8,128)(2,1)S(1)} copy(bf16[1,64,64]{0,2,1:T(8,128)(2,1)} %get-tuple-element.26) | data formatting | bytes 16384
  38.7 1.7 %copy.60 = bf16[1,64,64]{2,1,0:T(8,128)(2,1)S(1)} copy(bf16[1,64,64]{0,2,1:T(8,128)(2,1)} %get-tuple-element.25) | data formatting | bytes 16384
  40.4 0.5 copy.61
  40.9 1.7 %copy.62 = bf16[1,64,64]{2,1,0:T(8,128)(2,1)S(1)} copy(bf16[1,64,64]{0,2,1:T(8,128)(2,1)} %get-tuple-element.23) | data formatting | bytes 16384
  42.6 1.8 %copy.59 = bf16[1,64,64]{2,1,0:T(8,128)(2,1)S(1)} copy(bf16[1,64,64]{0,2,1:T(8,128)(2,1)} %get-tuple-element.19) | data formatting | bytes 16384
  44.3 1.7 %copy.56 = bf16[1,64,64]{2,1,0:T(8,128)(2,1)S(1)} copy(bf16[1,64,64]{0,2,1:T(8,128)(2,1)} %get-tuple-element.20) | data formatting | bytes 16384
  46.0 1.7 %copy.53 = bf16[1,64,64]{2,1,0:T(8,128)(2,1)S(1)} copy(bf16[1,64,64]{0,2,1:T(8,128)(2,1)} %get-tuple-element.21) | data formatting | bytes 16384
  47.7 1.7 %copy.50 = bf16[1,64,64]{2,1,0:T(8,128)(2,1)S(1)} copy(bf16[1,64,64]{0,2,1:T(8,128)(2,1)} %get-tuple-element.22) | data formatting | bytes 16384
  49.4 0.5 copy.47
  49.9 1.1 pad_maximum_fusion
  51.0 1.8 %copy.17 = bf16[128,40,128]{2,0,1:T(8,128)(2,1)S(1)} copy(bf16[128,40,128]{0,2,1:T(8,128)(2,1)} %bitcast.143) | data formatting | bytes 2621440 | tf_op jit(solution)/shard_map/reshape | solution.py:47
  52.8 0.5 convolution_bitcast_fusion
  53.3 14.4 %psum.7 = f32[128,64]{0,1:T(8,128)S(1)} all-reduce(f32[128,64]{0,1:T(8,128)S(1)} %convolution_bitcast_fusion), channel_id=1, replica_groups=mesh['leaf'=64,'blk'=4] {'blk'}, use_global_device_ids=true, to_apply=%region_0.2 | all-reduce | flops 8192 | bytes 65536 | tf_op jit(solution)/shard_map/psum | solution.py:53
  67.7 0.3 collective-permute-start.2
  68.0 1.7 %gather_fusion.4 = bf16[32,128,128]{2,1,0:T(8,128)(2,1)} fusion(bf16[40,128,128]{2,1,0:T(8,128)(2,1)S(1)} %bitcast.136, s32[1024]{0:T(1024)S(1)} %get-tuple-element.46), kind=kCustom, calls=%fused_computation.4.clone | custom fusion | bytes 2097280 | tf_op jit(solution)/shard_map/jit(_take)/gather | solution.py:58
  69.7 1.7 %gather_fusion.3 = bf16[32,128,128]{2,1,0:T(8,128)(2,1)} fusion(bf16[40,128,128]{2,1,0:T(8,128)(2,1)S(1)} %bitcast.137, s32[1024]{0:T(1024)S(1)} %get-tuple-element.47), kind=kCustom, calls=%fused_computation.3.clone | custom fusion | bytes 2097280 | tf_op jit(solution)/shard_map/jit(_take)/gather | solution.py:58
  71.3 0.7 gather_fusion.2
  72.1 1.7 %gather_fusion.1 = bf16[32,128,128]{2,1,0:T(8,128)(2,1)} fusion(bf16[40,128,128]{2,1,0:T(8,128)(2,1)S(1)} %bitcast.139, s32[1024]{0:T(1024)S(1)} %get-tuple-element.49), kind=kCustom, calls=%fused_computation.1.clone | custom fusion | bytes 2097280 | tf_op jit(solution)/shard_map/jit(_take)/gather | solution.py:58
  73.7 3.8 %fusion.3 = f32[32,128,128]{1,2,0:T(8,128)} fusion(bf16[32,128,128]{2,1,0:T(8,128)(2,1)} %gather_fusion.4, bf16[32,6,128,128]{3,2,1,0:T(8,128)(2,1)} %param.9, pred[32]{0:T(512)(128)(4,1)S(1)} %get-tuple-element.36), kind=kOutput, calls=%fused_computation.22 | convolution fusion | flops 134742016 | bytes 4194336 | tf_op jit(solution)/shard_map/crp,cpq->crq/dot_general | solution.py:59
  77.6 3.5 %fusion.5 = f32[32,128,128]{1,2,0:T(8,128)} fusion(bf16[32,128,128]{2,1,0:T(8,128)(2,1)S(1)} %copy-done.6, bf16[32,6,128,128]{3,2,1,0:T(8,128)(2,1)} %param.9, pred[32]{0:T(512)(128)(4,1)S(1)} %get-tuple-element.38), kind=kOutput, calls=%fused_computation.24 | convolution fusion | flops 134742016 | bytes 4194336 | tf_op jit(solution)/shard_map/crp,cpq->crq/dot_general | solution.py:59
  81.1 3.5 %fusion.7 = f32[32,128,128]{1,2,0:T(8,128)} fusion(bf16[32,128,128]{2,1,0:T(8,128)(2,1)S(1)} %gather_fusion.2, bf16[32,6,128,128]{3,2,1,0:T(8,128)(2,1)} %param.9, pred[32]{0:T(512)(128)(4,1)S(1)} %get-tuple-element.40), kind=kOutput, calls=%fused_computation.26 | convolution fusion | flops 134742016 | bytes 4194336 | tf_op jit(solution)/shard_map/crp,cpq->crq/dot_general | solution.py:59
  84.6 3.5 %fusion.9 = f32[32,128,128]{1,2,0:T(8,128)} fusion(bf16[32,128,128]{2,1,0:T(8,128)(2,1)S(1)} %copy-done.5, bf16[32,6,128,128]{3,2,1,0:T(8,128)(2,1)} %param.9, pred[32]{0:T(512)(128)(4,1)S(1)} %get-tuple-element.42), kind=kOutput, calls=%fused_computation.28 | convolution fusion | flops 134742016 | bytes 4194336 | tf_op jit(solution)/shard_map/crp,cpq->crq/dot_general | solution.py:59
  88.3 0.7 gather_fusion
  89.6 3.7 %collective-permute-done.3 = f32[128,64]{0,1:T(8,128)S(1)} collective-permute-done((f32[128,64]{0,1:T(8,128)S(1)}, f32[128,64]{0,1:T(8,128)S(1)}, u32[]{:S(2)}, u32[]{:S(2)}) %collective-permute-start.3) | collective-permute-done | bytes 32800 | tf_op jit(solution)/shard_map/ppermute | solution.py:30
  93.5 0.6 collective-permute-start.4
  94.3 4.1 %collective-permute-done.4 = f32[128,64]{0,1:T(8,128)S(1)} collective-permute-done((f32[128,64]{0,1:T(8,128)S(1)}, f32[128,64]{0,1:T(8,128)S(1)}, u32[]{:S(2)}, u32[]{:S(2)}) %collective-permute-start.4) | collective-permute-done | bytes 32800 | tf_op jit(solution)/shard_map/ppermute | solution.py:30
  98.6 4.6 %collective-permute-start.5 = (f32[128,64]{0,1:T(8,128)S(1)}, f32[128,64]{0,1:T(8,128)S(1)}, u32[]{:S(2)}, u32[]{:S(2)}) collective-permute-start(f32[128,64]{0,1:T(8,128)S(1)} %convolution_add_fusion.6), channel_id=1, source_target_pairs={{0,32},{4,36},{8,40},{12,44},{16,48},{20,52},{24,56},{28,60},{32,0... | collective-permute-start | bytes 98312 | tf_op jit(solution)/shard_map/ppermute | solution.py:30
  103.4 3.4 %collective-permute-done.5 = f32[128,64]{0,1:T(8,128)S(1)} collective-permute-done((f32[128,64]{0,1:T(8,128)S(1)}, f32[128,64]{0,1:T(8,128)S(1)}, u32[]{:S(2)}, u32[]{:S(2)}) %collective-permute-start.5) | collective-permute-done | bytes 32800 | tf_op jit(solution)/shard_map/ppermute | solution.py:30
  107.4 3.6 %collective-permute-done.6 = f32[128,64]{0,1:T(8,128)S(1)} collective-permute-done((f32[128,64]{0,1:T(8,128)S(1)}, f32[128,64]{0,1:T(8,128)S(1)}, u32[]{:S(2)}, u32[]{:S(2)}) %collective-permute-start.6) | collective-permute-done | bytes 32800 | tf_op jit(solution)/shard_map/ppermute | solution.py:30
  111.3 2.4 %collective-permute-start.7 = (f32[128,64]{1,0:T(8,128)S(1)}, f32[128,64]{1,0:T(8,128)S(1)}, u32[]{:S(2)}, u32[]{:S(2)}) collective-permute-start(f32[128,64]{1,0:T(8,128)S(1)} %convolution_add_fusion), channel_id=1, source_target_pairs={{0,128},{4,132},{8,136},{12,140},{16,144},{20,148},{24,152},{28,15... | collective-permute-start | bytes 98312 | tf_op jit(solution)/shard_map/ppermute | solution.py:30
  113.7 3.5 %fusion.11 = f32[32,128,128]{1,2,0:T(8,128)} fusion(bf16[32,128,128]{2,1,0:T(8,128)(2,1)S(1)} %gather_fusion, bf16[32,6,128,128]{3,2,1,0:T(8,128)(2,1)} %param.9, pred[32]{0:T(512)(128)(4,1)S(1)} %get-tuple-element.44), kind=kOutput, calls=%fused_computation.30 | convolution fusion | flops 134742016 | bytes 4194336 | tf_op jit(solution)/shard_map/crp,cpq->crq/dot_general | solution.py:59
  117.2 1.8 %gather_fusion.5 = bf16[32,128,128]{2,1,0:T(8,128)(2,1)} fusion(bf16[40,128,128]{2,1,0:T(8,128)(2,1)S(1)} %bitcast.141, s32[1024]{0:T(1024)S(1)} %pad_clamp_fusion), kind=kCustom, calls=%fused_computation.5.clone | custom fusion | bytes 2097280 | tf_op jit(solution)/shard_map/jit(_take)/gather | solution.py:58
  119.8 0.3 convolution_add_fusion.2
  121.3 0.5 fusion.77
  121.9 4.7 %bitcast_add_fusion = f32[128,32,128]{0,2,1:T(8,128)S(1)} fusion(f32[128,32,128]{0,2,1:T(8,128)S(1)} %fusion.77, f32[32,128,128]{1,2,0:T(8,128)S(1)} %copy-done.3, f32[32,128,128]{1,2,0:T(8,128)S(1)} %copy-done.4, f32[32,128,128]{1,2,0:T(8,128)} %fusion.7, f32[32,128,128]{1,2,0:T(8,128)} %fusion.11, f32[32,128,128]{1,2,0:T(8,128)} %fusion.9, ...), kind=kOutput, calls=%fused_computation.6 | convolution fusion | flops 137887744 | bytes 16777248 | tf_op jit(solution)/shard_map/crp,cpq->crq/dot_general | solution.py:59
  126.6 1.8 %copy.40 = f32[128,4096]{1,0:T(8,128)} copy(f32[128,4096]{0,1:T(8,128)S(1)} %bitcast.142) | data formatting | bytes 4194304 | tf_op jit(solution)/shard_map/reshape | solution.py:88
  (51 shorter events, 4.5 us)
Async XLA Ops:
  0.0 52.8 %copy-start = (bf16[32,64,128]{2,1,0:T(8,128)(2,1)S(1)}, bf16[32,64,128]{2,1,0:T(8,128)(2,1)}, u32[]{:S(2)}) copy-start(bf16[32,64,128]{2,1,0:T(8,128)(2,1)} %param.11) | copy-start | bytes 1572868
  0.0 13.4 %copy-start.8 = (s32[32,6]{0,1:T(8,128)S(1)}, s32[32,6]{0,1:T(8,128)}, u32[]{:S(2)}) copy-start(s32[32,6]{0,1:T(8,128)} %param.10) | copy-start | bytes 2308
  0.0 13.5 %copy-start.2 = (bf16[126,64,64]{0,2,1:T(8,128)(2,1)S(1)}, bf16[126,64,64]{0,2,1:T(8,128)(2,1)}, u32[]{:S(2)}) copy-start(bf16[126,64,64]{0,2,1:T(8,128)(2,1)} %param.13) | copy-start | bytes 3096580
  1.8 48.1 %collective-permute-start = (bf16[128,512]{0,1:T(8,128)(2,1)S(1)}, bf16[128,512]{0,1:T(8,128)(2,1)S(1)}, u32[]{:S(2)}, u32[]{:S(2)}) collective-permute-start(bf16[128,512]{0,1:T(8,128)(2,1)S(1)} %get-tuple-element.34), channel_id=1, source_target_pairs={{0,1},{1,2},{2,3},{3,4},{4,5},{5,6},{6,7},{7,8},{8,9},{9,10},{10,1... | collective-permute-start | bytes 393224 | tf_op jit(solution)/shard_map/ppermute | solution.py:18
  5.3 44.6 %collective-permute-start.1 = (bf16[128,512]{0,1:T(8,128)(2,1)S(1)}, bf16[128,512]{0,1:T(8,128)(2,1)S(1)}, u32[]{:S(2)}, u32[]{:S(2)}) collective-permute-start(bf16[128,512]{0,1:T(8,128)(2,1)S(1)} %get-tuple-element.35), channel_id=1, source_target_pairs={{1,0},{2,1},{3,2},{4,3},{5,4},{6,5},{7,6},{8,7},{9,8},{10,9},{11,1... | collective-permute-start | bytes 393224 | tf_op jit(solution)/shard_map/ppermute | solution.py:20
  13.5 4.7 %copy-start.1 = (bf16[126,64,64]{0,2,1:T(8,128)(2,1)S(1)}, bf16[126,64,64]{0,2,1:T(8,128)(2,1)}, u32[]{:S(2)}) copy-start(bf16[126,64,64]{0,2,1:T(8,128)(2,1)} %param.12) | copy-start | bytes 3096580
  42.6 6.8 %copy-start.7 = (bf16[1,64,64]{0,2,1:T(8,128)(2,1)S(1)}, bf16[1,64,64]{0,2,1:T(8,128)(2,1)}, u32[]{:S(2)}) copy-start(bf16[1,64,64]{0,2,1:T(8,128)(2,1)} %get-tuple-element.18) | copy-start | bytes 24580
  67.7 21.3 %collective-permute-start.2 = (f32[128,64]{0,1:T(8,128)S(1)}, f32[128,64]{0,1:T(8,128)S(1)}, u32[]{:S(2)}, u32[]{:S(2)}) collective-permute-start(f32[128,64]{0,1:T(8,128)S(1)} %psum.7), channel_id=1, source_target_pairs={{0,4},{4,0},{8,12},{12,8},{16,20},{20,16},{24,28},{28,24},{32,36},... | collective-permute-start | bytes 98312 | tf_op jit(solution)/shard_map/ppermute | solution.py:30
  73.7 3.9 %copy-start.6 = (bf16[32,128,128]{2,1,0:T(8,128)(2,1)S(1)}, bf16[32,128,128]{2,1,0:T(8,128)(2,1)}, u32[]{:S(2)}) copy-start(bf16[32,128,128]{2,1,0:T(8,128)(2,1)} %gather_fusion.3) | copy-start | bytes 3145732
  81.1 3.5 %copy-start.5 = (bf16[32,128,128]{2,1,0:T(8,128)(2,1)S(1)}, bf16[32,128,128]{2,1,0:T(8,128)(2,1)}, u32[]{:S(2)}) copy-start(bf16[32,128,128]{2,1,0:T(8,128)(2,1)} %gather_fusion.1) | copy-start | bytes 3145732
  89.3 4.0 %collective-permute-start.3 = (f32[128,64]{0,1:T(8,128)S(1)}, f32[128,64]{0,1:T(8,128)S(1)}, u32[]{:S(2)}, u32[]{:S(2)}) collective-permute-start(f32[128,64]{0,1:T(8,128)S(1)} %convolution_add_fusion.8), channel_id=1, source_target_pairs={{0,8},{4,12},{8,0},{12,4},{16,24},{20,28},{24,16},{28,20},{32,40},... | collective-permute-start | bytes 98312 | tf_op jit(solution)/shard_map/ppermute | solution.py:30
  93.5 4.9 %collective-permute-start.4 = (f32[128,64]{0,1:T(8,128)S(1)}, f32[128,64]{0,1:T(8,128)S(1)}, u32[]{:S(2)}, u32[]{:S(2)}) collective-permute-start(f32[128,64]{0,1:T(8,128)S(1)} %convolution_add_fusion.7), channel_id=1, source_target_pairs={{0,16},{4,20},{8,24},{12,28},{16,0},{20,4},{24,8},{28,12},{32,48},... | collective-permute-start | bytes 98312 | tf_op jit(solution)/shard_map/ppermute | solution.py:30
  98.6 8.3 %collective-permute-start.5 = (f32[128,64]{0,1:T(8,128)S(1)}, f32[128,64]{0,1:T(8,128)S(1)}, u32[]{:S(2)}, u32[]{:S(2)}) collective-permute-start(f32[128,64]{0,1:T(8,128)S(1)} %convolution_add_fusion.6), channel_id=1, source_target_pairs={{0,32},{4,36},{8,40},{12,44},{16,48},{20,52},{24,56},{28,60},{32,0... | collective-permute-start | bytes 98312 | tf_op jit(solution)/shard_map/ppermute | solution.py:30
  107.1 4.0 %collective-permute-start.6 = (f32[128,64]{0,1:T(8,128)S(1)}, f32[128,64]{0,1:T(8,128)S(1)}, u32[]{:S(2)}, u32[]{:S(2)}) collective-permute-start(f32[128,64]{0,1:T(8,128)S(1)} %convolution_add_fusion.5), channel_id=1, source_target_pairs={{0,64},{4,68},{8,72},{12,76},{16,80},{20,84},{24,88},{28,92},{32,9... | collective-permute-start | bytes 98312 | tf_op jit(solution)/shard_map/ppermute | solution.py:30
  111.3 7.6 %collective-permute-start.7 = (f32[128,64]{1,0:T(8,128)S(1)}, f32[128,64]{1,0:T(8,128)S(1)}, u32[]{:S(2)}, u32[]{:S(2)}) collective-permute-start(f32[128,64]{1,0:T(8,128)S(1)} %convolution_add_fusion), channel_id=1, source_target_pairs={{0,128},{4,132},{8,136},{12,140},{16,144},{20,148},{24,152},{28,15... | collective-permute-start | bytes 98312 | tf_op jit(solution)/shard_map/ppermute | solution.py:30
  119.0 2.9 %copy-start.4 = (f32[32,128,128]{1,2,0:T(8,128)S(1)}, f32[32,128,128]{1,2,0:T(8,128)}, u32[]{:S(2)}) copy-start(f32[32,128,128]{1,2,0:T(8,128)} %fusion.5) | copy-start | bytes 6291460
  119.1 2.8 %copy-start.3 = (f32[32,128,128]{1,2,0:T(8,128)S(1)}, f32[32,128,128]{1,2,0:T(8,128)}, u32[]{:S(2)}) copy-start(f32[32,128,128]{1,2,0:T(8,128)} %fusion.3) | copy-start | bytes 6291460
where the time goes:
time: 129 us; the launch traced here: 128 us
  local copies, waits for them, and re-layouts  49.9 us (39%)
  matrix products  28 us (22%)
  starting transfers between devices  19.6 us (15%)
  waiting for transfers between devices  14.8 us (11%)
  blocking collectives  14.4 us (11%)
    unnamed x35, local copies, waits for them, and re-layouts  26.3 us
    dot_general x6, matrix products, body(): jnp.einsum('crp,cpq->crq', picked, near_blocks[:, slot], preferred_elemen...  22.5 us
    ppermute x6, waiting for transfers between devices, from_partner(): return lax.ppermute(value, axis, pairs)  14.8 us
    psum x1, blocking collectives, body(): moment = lax.psum(partial_value, 'blk')  14.4 us
    dynamic_slice x2, local copies, waits for them, and re-layouts, pick_matrix(): lax.dynamic_index_in_dim(table, table_row, 0, keepdims=False)  11.8 us
    gather x6, local copies, waits for them, and re-layouts, body(): picked = jnp.take(by_cluster, local_columns[:, slot], axis=0)  8.24 us
    ppermute x6, starting transfers between devices, from_partner(): return lax.ppermute(value, axis, pairs)  8.07 us
    ppermute x1, starting transfers between devices, padded(): lax.ppermute(head, axis, [((i + 1) % count, i) for i in range(ends)])  8.06 us
  transfers between devices with their start and end apart: 8, of which 4 were waited for; matrix products, arithmetic and copies ran while one was open for 49% of the time, Pallas kernels for 0%

commit v1 on v0

--- a/solution.py
+++ b/solution.py
@@ -50,7 +50,9 @@
     partial_value = jnp.einsum(
         "crp,ckp->rk", own_sources, basis, preferred_element_type=jnp.float32
     )
-    moment = lax.psum(partial_value, "blk")
+    moment = partial_value
+    for hop in (1, 2):
+        moment = moment + lax.ppermute(moment, "blk", [(dev, dev ^ hop) for dev in range(4)])
     first_cluster = lax.axis_index(("leaf", "blk")) * own_clusters
     local_columns = near_cols - (first_cluster - REACH)
     near = jnp.zeros((own_clusters, rhs_count, panel_size), jnp.float32)

time: 129 us -> 115 us (0.89); the launches traced: 128 us -> 113 us
  blocking collectives: 14.4 us -> 0 us
  local copies, waits for them, and re-layouts: 49.9 us -> 48.1 us
    psum x1 -> x0, blocking collectives: 14.4 us -> none  [body(): moment = lax.psum(partial_value, 'blk')]
    gather x6, local copies, waits for them, and re-layouts: 8.24 us -> 6.4 us  [body(): picked = jnp.take(by_cluster, local_columns[:, slot], axis=0)]
    unnamed x35 -> x33, local copies, waits for them, and re-layouts: 26.3 us -> 26.3 us
  transfers between devices with their start and end apart: 8 -> 10, of which waited for: 4 -> 5; matrix products, arithmetic and copies ran while one was open for 49% -> 54% of each run, Pallas kernels for 0% -> 0%
where the time goes in v1:
time: 115 us; the launch traced here: 113 us
  local copies, waits for them, and re-layouts  48.1 us (42%)
  matrix products  27.6 us (24%)
  starting transfers between devices  20.7 us (18%)
  waiting for transfers between devices  14.9 us (13%)
  other arithmetic  1.2 us (1%)
    unnamed x33, local copies, waits for them, and re-layouts  26.3 us
    dot_general x6, matrix products, body(): jnp.einsum('crp,cpq->crq', picked, near_blocks[:, slot], preferred_elemen...  22.1 us
    ppermute x6, waiting for transfers between devices, from_partner(): return lax.ppermute(value, axis, pairs)  13.6 us
    dynamic_slice x2, local copies, waits for them, and re-layouts, pick_matrix(): lax.dynamic_index_in_dim(table, table_row, 0, keepdims=False)  11.8 us
    ppermute x6, starting transfers between devices, from_partner(): return lax.ppermute(value, axis, pairs)  8.79 us
    ppermute x1, starting transfers between devices, padded(): lax.ppermute(head, axis, [((i + 1) % count, i) for i in range(ends)])  8.06 us
    gather x6, local copies, waits for them, and re-layouts, body(): picked = jnp.take(by_cluster, local_columns[:, slot], axis=0)  6.4 us
    ppermute x1, starting transfers between devices, padded(): lax.ppermute(tail, axis, [(i, (i + 1) % count) for i in range(ends)])  3.48 us
  transfers between devices with their start and end apart: 10, of which 5 were waited for; matrix products, arithmetic and copies ran while one was open for 54% of the time, Pallas kernels for 0%

profile of v1, /device:TPU:2, one launch (start us, length us, event | category | flops | bytes accessed | tf_op | source)
XLA Modules:
  0.0 112.9 jit_solution(6110118758286980433)
XLA Ops:
  0.0 1.7 %copy.14 = bf16[128,4096]{0,1:T(8,128)(2,1)S(1)} copy(bf16[128,4096]{1,0:T(8,128)(2,1)} %param.8) | data formatting | bytes 2097152 | tf_op args[0]
  1.8 3.5 %collective-permute-start = (bf16[128,512]{0,1:T(8,128)(2,1)S(1)}, bf16[128,512]{0,1:T(8,128)(2,1)S(1)}, u32[]{:S(2)}, u32[]{:S(2)}) collective-permute-start(bf16[128,512]{0,1:T(8,128)(2,1)S(1)} %get-tuple-element.34), channel_id=1, source_target_pairs={{0,1},{1,2},{2,3},{3,4},{4,5},{5,6},{6,7},{7,8},{8,9},{9,10},{10,1... | collective-permute-start | bytes 393224 | tf_op jit(solution)/shard_map/ppermute | solution.py:18
  5.3 8.1 %collective-permute-start.1 = (bf16[128,512]{0,1:T(8,128)(2,1)S(1)}, bf16[128,512]{0,1:T(8,128)(2,1)S(1)}, u32[]{:S(2)}, u32[]{:S(2)}) collective-permute-start(bf16[128,512]{0,1:T(8,128)(2,1)S(1)} %get-tuple-element.35), channel_id=1, source_target_pairs={{1,0},{2,1},{3,2},{4,3},{5,4},{6,5},{7,6},{8,7},{9,8},{10,9},{11,1... | collective-permute-start | bytes 393224 | tf_op jit(solution)/shard_map/ppermute | solution.py:20
  13.5 4.6 %constant_dynamic-slice_fusion.15 = (bf16[1,64,64]{0,2,1:T(8,128)(2,1)}, bf16[1,64,64]{0,2,1:T(8,128)(2,1)}, bf16[1,64,64]{0,2,1:T(8,128)(2,1)}, bf16[1,64,64]{0...) fusion(bf16[126,64,64]{0,2,1:T(8,128)(2,1)S(1)} %copy-done.2, s32[]{:T(128)S(6)} %select_n.51, ...), kind=kLoop, calls=%fused_computation.109 | loop fusion | bytes 98328 | tf_op jit(solution)/shard_map/jit(dynamic_index_in_dim)/dynamic_slice | solution.py:34
  18.1 7.1 %constant_dynamic-slice_fusion.1 = (bf16[1,64,64]{0,2,1:T(8,128)(2,1)S(1)}, bf16[1,64,64]{0,2,1:T(8,128)(2,1)}, bf16[1,64,64]{0,2,1:T(8,128)(2,1)}, bf16[1,64,64...) fusion(bf16[126,64,64]{0,2,1:T(8,128)(2,1)S(1)} %copy-done.1, ...), kind=kLoop, calls=%fused_computation.95 | loop fusion | bytes 163880 | tf_op jit(solution)/shard_map/jit(dynamic_index_in_dim)/dynamic_slice | solution.py:34
  25.3 1.7 %copy.49 = bf16[1,64,64]{2,1,0:T(8,128)(2,1)S(1)} copy(bf16[1,64,64]{0,2,1:T(8,128)(2,1)} %get-tuple-element.32) | data formatting | bytes 16384
  27.0 1.7 %copy.48 = bf16[1,64,64]{2,1,0:T(8,128)(2,1)S(1)} copy(bf16[1,64,64]{0,2,1:T(8,128)(2,1)} %get-tuple-element.33) | data formatting | bytes 16384
  28.6 1.7 %copy.51 = bf16[1,64,64]{2,1,0:T(8,128)(2,1)S(1)} copy(bf16[1,64,64]{0,2,1:T(8,128)(2,1)} %get-tuple-element.31) | data formatting | bytes 16384
  30.3 1.7 %copy.52 = bf16[1,64,64]{2,1,0:T(8,128)(2,1)S(1)} copy(bf16[1,64,64]{0,2,1:T(8,128)(2,1)} %get-tuple-element.30) | data formatting | bytes 16384
  32.0 1.7 %copy.54 = bf16[1,64,64]{2,1,0:T(8,128)(2,1)S(1)} copy(bf16[1,64,64]{0,2,1:T(8,128)(2,1)} %get-tuple-element.29) | data formatting | bytes 16384
  33.7 1.7 %copy.55 = bf16[1,64,64]{2,1,0:T(8,128)(2,1)S(1)} copy(bf16[1,64,64]{0,2,1:T(8,128)(2,1)} %get-tuple-element.28) | data formatting | bytes 16384
  35.4 1.7 %copy.57 = bf16[1,64,64]{2,1,0:T(8,128)(2,1)S(1)} copy(bf16[1,64,64]{0,2,1:T(8,128)(2,1)} %get-tuple-element.27) | data formatting | bytes 16384
  37.0 1.7 %copy.58 = bf16[1,64,64]{2,1,0:T(8,128)(2,1)S(1)} copy(bf16[1,64,64]{0,2,1:T(8,128)(2,1)} %get-tuple-element.26) | data formatting | bytes 16384
  38.7 1.7 %copy.60 = bf16[1,64,64]{2,1,0:T(8,128)(2,1)S(1)} copy(bf16[1,64,64]{0,2,1:T(8,128)(2,1)} %get-tuple-element.25) | data formatting | bytes 16384
  40.4 0.5 copy.61
  40.9 1.7 %copy.62 = bf16[1,64,64]{2,1,0:T(8,128)(2,1)S(1)} copy(bf16[1,64,64]{0,2,1:T(8,128)(2,1)} %get-tuple-element.23) | data formatting | bytes 16384
  42.6 1.8 %copy.59 = bf16[1,64,64]{2,1,0:T(8,128)(2,1)S(1)} copy(bf16[1,64,64]{0,2,1:T(8,128)(2,1)} %get-tuple-element.19) | data formatting | bytes 16384
  44.3 1.7 %copy.56 = bf16[1,64,64]{2,1,0:T(8,128)(2,1)S(1)} copy(bf16[1,64,64]{0,2,1:T(8,128)(2,1)} %get-tuple-element.20) | data formatting | bytes 16384
  46.0 1.7 %copy.53 = bf16[1,64,64]{2,1,0:T(8,128)(2,1)S(1)} copy(bf16[1,64,64]{0,2,1:T(8,128)(2,1)} %get-tuple-element.21) | data formatting | bytes 16384
  47.7 1.7 %copy.50 = bf16[1,64,64]{2,1,0:T(8,128)(2,1)S(1)} copy(bf16[1,64,64]{0,2,1:T(8,128)(2,1)} %get-tuple-element.22) | data formatting | bytes 16384
  49.4 0.5 copy.47
  49.9 1.1 %pad_maximum_fusion = bf16[128,5120]{0,1:T(8,128)(2,1)} fusion(bf16[128,512]{0,1:T(8,128)(2,1)S(1)} %collective-permute-done.1, bf16[128,4096]{0,1:T(8,128)(2,1)S(1)} %copy.14, bf16[128,512]{0,1:T(8,128)(2,1)S(1)} %collective-permute-done), kind=kLoop, calls=%fused_computation.7 | loop fusion | flops 3932160 | bytes 2621440 | tf_op jit(solution)/shard_map/concatenate | solution.py:16
  51.0 1.8 %copy.17 = bf16[128,40,128]{2,0,1:T(8,128)(2,1)S(1)} copy(bf16[128,40,128]{0,2,1:T(8,128)(2,1)} %bitcast.143) | data formatting | bytes 2621440 | tf_op jit(solution)/shard_map/reshape | solution.py:47
  52.8 0.5 convolution_bitcast_fusion
  53.3 0.3 collective-permute-start.2
  53.6 0.7 gather_fusion.4
  54.3 1.7 %gather_fusion.3 = bf16[32,128,128]{2,1,0:T(8,128)(2,1)} fusion(bf16[40,128,128]{2,1,0:T(8,128)(2,1)S(1)} %bitcast.137, s32[1024]{0:T(1024)S(1)} %get-tuple-element.47), kind=kCustom, calls=%fused_computation.3.clone | custom fusion | bytes 2097280 | tf_op jit(solution)/shard_map/jit(_take)/gather | solution.py:60
  56.0 3.5 %fusion.3 = f32[32,128,128]{1,2,0:T(8,128)} fusion(bf16[32,128,128]{2,1,0:T(8,128)(2,1)S(1)} %gather_fusion.4, bf16[32,6,128,128]{3,2,1,0:T(8,128)(2,1)} %param.9, pred[32]{0:T(512)(128)(4,1)S(1)} %get-tuple-element.36), kind=kOutput, calls=%fused_computation.22 | convolution fusion | flops 134742016 | bytes 4194336 | tf_op jit(solution)/shard_map/crp,cpq->crq/dot_general | solution.py:61
  59.5 3.5 %fusion.5 = f32[32,128,128]{1,2,0:T(8,128)} fusion(bf16[32,128,128]{2,1,0:T(8,128)(2,1)S(1)} %copy-done.5, bf16[32,6,128,128]{3,2,1,0:T(8,128)(2,1)} %param.9, pred[32]{0:T(512)(128)(4,1)S(1)} %get-tuple-element.38), kind=kOutput, calls=%fused_computation.24 | convolution fusion | flops 134742016 | bytes 4194336 | tf_op jit(solution)/shard_map/crp,cpq->crq/dot_general | solution.py:61
  63.0 0.7 gather_fusion.2
  63.9 3.4 %fusion.7 = f32[32,128,128]{1,2,0:T(8,128)} fusion(bf16[32,128,128]{2,1,0:T(8,128)(2,1)S(1)} %gather_fusion.2, bf16[32,6,128,128]{3,2,1,0:T(8,128)(2,1)} %param.9, pred[32]{0:T(512)(128)(4,1)S(1)} %get-tuple-element.40), kind=kOutput, calls=%fused_computation.26 | convolution fusion | flops 134742016 | bytes 4194336 | tf_op jit(solution)/shard_map/crp,cpq->crq/dot_general | solution.py:61
  67.3 0.7 gather_fusion.1
  68.0 1.2 %collective-permute-done.3 = f32[128,64]{0,1:T(8,128)S(1)} collective-permute-done((f32[128,64]{0,1:T(8,128)S(1)}, f32[128,64]{0,1:T(8,128)S(1)}, u32[]{:S(2)}, u32[]{:S(2)}) %collective-permute-start.3) | collective-permute-done | bytes 32800 | tf_op jit(solution)/shard_map/ppermute | solution.py:55
  69.3 3.5 %fusion.9 = f32[32,128,128]{1,2,0:T(8,128)} fusion(bf16[32,128,128]{2,1,0:T(8,128)(2,1)S(1)} %gather_fusion.1, bf16[32,6,128,128]{3,2,1,0:T(8,128)(2,1)} %param.9, pred[32]{0:T(512)(128)(4,1)S(1)} %get-tuple-element.42), kind=kOutput, calls=%fused_computation.28 | convolution fusion | flops 134742016 | bytes 4194336 | tf_op jit(solution)/shard_map/crp,cpq->crq/dot_general | solution.py:61
  72.8 0.7 gather_fusion
  74.3 3.7 %collective-permute-done.5 = f32[128,64]{0,1:T(8,128)S(1)} collective-permute-done((f32[128,64]{0,1:T(8,128)S(1)}, f32[128,64]{0,1:T(8,128)S(1)}, u32[]{:S(2)}, u32[]{:S(2)}) %collective-permute-start.5) | collective-permute-done | bytes 32800 | tf_op jit(solution)/shard_map/ppermute | solution.py:30
  78.2 1.2 %collective-permute-start.6 = (f32[128,64]{0,1:T(8,128)S(1)}, f32[128,64]{0,1:T(8,128)S(1)}, u32[]{:S(2)}, u32[]{:S(2)}) collective-permute-start(f32[128,64]{0,1:T(8,128)S(1)} %convolution_add_fusion.7), channel_id=1, source_target_pairs={{0,16},{4,20},{8,24},{12,28},{16,0},{20,4},{24,8},{28,12},{32,48},... | collective-permute-start | bytes 98312 | tf_op jit(solution)/shard_map/ppermute | solution.py:30
  79.6 3.5 %collective-permute-done.6 = f32[128,64]{0,1:T(8,128)S(1)} collective-permute-done((f32[128,64]{0,1:T(8,128)S(1)}, f32[128,64]{0,1:T(8,128)S(1)}, u32[]{:S(2)}, u32[]{:S(2)}) %collective-permute-start.6) | collective-permute-done | bytes 32800 | tf_op jit(solution)/shard_map/ppermute | solution.py:30
  83.3 4.9 %collective-permute-start.7 = (f32[128,64]{0,1:T(8,128)S(1)}, f32[128,64]{0,1:T(8,128)S(1)}, u32[]{:S(2)}, u32[]{:S(2)}) collective-permute-start(f32[128,64]{0,1:T(8,128)S(1)} %convolution_add_fusion.6), channel_id=1, source_target_pairs={{0,32},{4,36},{8,40},{12,44},{16,48},{20,52},{24,56},{28,60},{32,0... | collective-permute-start | bytes 98312 | tf_op jit(solution)/shard_map/ppermute | solution.py:30
  88.4 2.8 %collective-permute-done.7 = f32[128,64]{0,1:T(8,128)S(1)} collective-permute-done((f32[128,64]{0,1:T(8,128)S(1)}, f32[128,64]{0,1:T(8,128)S(1)}, u32[]{:S(2)}, u32[]{:S(2)}) %collective-permute-start.7) | collective-permute-done | bytes 32800 | tf_op jit(solution)/shard_map/ppermute | solution.py:30
  91.8 3.6 %collective-permute-done.8 = f32[128,64]{0,1:T(8,128)S(1)} collective-permute-done((f32[128,64]{0,1:T(8,128)S(1)}, f32[128,64]{0,1:T(8,128)S(1)}, u32[]{:S(2)}, u32[]{:S(2)}) %collective-permute-start.8) | collective-permute-done | bytes 32800 | tf_op jit(solution)/shard_map/ppermute | solution.py:30
  95.7 2.5 %collective-permute-start.9 = (f32[128,64]{1,0:T(8,128)S(1)}, f32[128,64]{1,0:T(8,128)S(1)}, u32[]{:S(2)}, u32[]{:S(2)}) collective-permute-start(f32[128,64]{1,0:T(8,128)S(1)} %convolution_add_fusion), channel_id=1, source_target_pairs={{0,128},{4,132},{8,136},{12,140},{16,144},{20,148},{24,152},{28,15... | collective-permute-start | bytes 98312 | tf_op jit(solution)/shard_map/ppermute | solution.py:30
  98.2 3.5 %fusion.11 = f32[32,128,128]{1,2,0:T(8,128)} fusion(bf16[32,128,128]{2,1,0:T(8,128)(2,1)S(1)} %gather_fusion, bf16[32,6,128,128]{3,2,1,0:T(8,128)(2,1)} %param.9, pred[32]{0:T(512)(128)(4,1)S(1)} %get-tuple-element.44), kind=kOutput, calls=%fused_computation.30 | convolution fusion | flops 134742016 | bytes 4194336 | tf_op jit(solution)/shard_map/crp,cpq->crq/dot_general | solution.py:61
  101.7 1.7 %gather_fusion.5 = bf16[32,128,128]{2,1,0:T(8,128)(2,1)} fusion(bf16[40,128,128]{2,1,0:T(8,128)(2,1)S(1)} %bitcast.141, s32[1024]{0:T(1024)S(1)} %pad_clamp_fusion), kind=kCustom, calls=%fused_computation.5.clone | custom fusion | bytes 2097280 | tf_op jit(solution)/shard_map/jit(_take)/gather | solution.py:60
  104.2 0.3 convolution_add_fusion.2
  105.8 0.5 fusion.77
  106.4 4.7 %bitcast_add_fusion = f32[128,32,128]{0,2,1:T(8,128)S(1)} fusion(f32[128,32,128]{0,2,1:T(8,128)S(1)} %fusion.77, f32[32,128,128]{1,2,0:T(8,128)S(1)} %copy-done.3, f32[32,128,128]{1,2,0:T(8,128)S(1)} %copy-done.4, f32[32,128,128]{1,2,0:T(8,128)} %fusion.7, f32[32,128,128]{1,2,0:T(8,128)} %fusion.11, f32[32,128,128]{1,2,0:T(8,128)} %fusion.9, ...), kind=kOutput, calls=%fused_computation.6 | convolution fusion | flops 137887744 | bytes 16777248 | tf_op jit(solution)/shard_map/crp,cpq->crq/dot_general | solution.py:61
  111.1 1.8 %copy.40 = f32[128,4096]{1,0:T(8,128)} copy(f32[128,4096]{0,1:T(8,128)S(1)} %bitcast.142) | data formatting | bytes 4194304 | tf_op jit(solution)/shard_map/reshape | solution.py:90
  (54 shorter events, 4.6 us)
Async XLA Ops:
  0.0 52.8 %copy-start = (bf16[32,64,128]{2,1,0:T(8,128)(2,1)S(1)}, bf16[32,64,128]{2,1,0:T(8,128)(2,1)}, u32[]{:S(2)}) copy-start(bf16[32,64,128]{2,1,0:T(8,128)(2,1)} %param.11) | copy-start | bytes 1572868
  0.0 13.4 %copy-start.7 = (s32[32,6]{0,1:T(8,128)S(1)}, s32[32,6]{0,1:T(8,128)}, u32[]{:S(2)}) copy-start(s32[32,6]{0,1:T(8,128)} %param.10) | copy-start | bytes 2308
  0.0 13.5 %copy-start.2 = (bf16[126,64,64]{0,2,1:T(8,128)(2,1)S(1)}, bf16[126,64,64]{0,2,1:T(8,128)(2,1)}, u32[]{:S(2)}) copy-start(bf16[126,64,64]{0,2,1:T(8,128)(2,1)} %param.13) | copy-start | bytes 3096580
  1.8 48.1 %collective-permute-start = (bf16[128,512]{0,1:T(8,128)(2,1)S(1)}, bf16[128,512]{0,1:T(8,128)(2,1)S(1)}, u32[]{:S(2)}, u32[]{:S(2)}) collective-permute-start(bf16[128,512]{0,1:T(8,128)(2,1)S(1)} %get-tuple-element.34), channel_id=1, source_target_pairs={{0,1},{1,2},{2,3},{3,4},{4,5},{5,6},{6,7},{7,8},{8,9},{9,10},{10,1... | collective-permute-start | bytes 393224 | tf_op jit(solution)/shard_map/ppermute | solution.py:18
  5.3 44.6 %collective-permute-start.1 = (bf16[128,512]{0,1:T(8,128)(2,1)S(1)}, bf16[128,512]{0,1:T(8,128)(2,1)S(1)}, u32[]{:S(2)}, u32[]{:S(2)}) collective-permute-start(bf16[128,512]{0,1:T(8,128)(2,1)S(1)} %get-tuple-element.35), channel_id=1, source_target_pairs={{1,0},{2,1},{3,2},{4,3},{5,4},{6,5},{7,6},{8,7},{9,8},{10,9},{11,1... | collective-permute-start | bytes 393224 | tf_op jit(solution)/shard_map/ppermute | solution.py:20
  13.5 4.6 %copy-start.1 = (bf16[126,64,64]{0,2,1:T(8,128)(2,1)S(1)}, bf16[126,64,64]{0,2,1:T(8,128)(2,1)}, u32[]{:S(2)}) copy-start(bf16[126,64,64]{0,2,1:T(8,128)(2,1)} %param.12) | copy-start | bytes 3096580
  42.6 6.8 %copy-start.6 = (bf16[1,64,64]{0,2,1:T(8,128)(2,1)S(1)}, bf16[1,64,64]{0,2,1:T(8,128)(2,1)}, u32[]{:S(2)}) copy-start(bf16[1,64,64]{0,2,1:T(8,128)(2,1)} %get-tuple-element.18) | copy-start | bytes 24580
  53.3 10.5 %collective-permute-start.2 = (f32[128,64]{0,1:T(8,128)S(1)}, f32[128,64]{0,1:T(8,128)S(1)}, u32[]{:S(2)}, u32[]{:S(2)}) collective-permute-start(f32[128,64]{0,1:T(8,128)S(1)} %convolution_bitcast_fusion), channel_id=1, source_target_pairs={{0,1},{1,0},{2,3},{3,2},{4,5},{5,4},{6,7},{7,6},{8,9},{9,8},{10,11... | collective-permute-start | bytes 98312 | tf_op jit(solution)/shard_map/ppermute | solution.py:55
  56.0 3.5 %copy-start.5 = (bf16[32,128,128]{2,1,0:T(8,128)(2,1)S(1)}, bf16[32,128,128]{2,1,0:T(8,128)(2,1)}, u32[]{:S(2)}) copy-start(bf16[32,128,128]{2,1,0:T(8,128)(2,1)} %gather_fusion.3) | copy-start | bytes 3145732
  63.8 5.5 %collective-permute-start.3 = (f32[128,64]{0,1:T(8,128)S(1)}, f32[128,64]{0,1:T(8,128)S(1)}, u32[]{:S(2)}, u32[]{:S(2)}) collective-permute-start(f32[128,64]{0,1:T(8,128)S(1)} %add.187), channel_id=1, source_target_pairs={{0,2},{1,3},{2,0},{3,1},{4,6},{5,7},{6,4},{7,5},{8,10},{9,11},{10,... | collective-permute-start | bytes 98312 | tf_op jit(solution)/shard_map/ppermute | solution.py:55
  69.3 4.3 %collective-permute-start.4 = (f32[128,64]{0,1:T(8,128)S(1)}, f32[128,64]{0,1:T(8,128)S(1)}, u32[]{:S(2)}, u32[]{:S(2)}) collective-permute-start(f32[128,64]{0,1:T(8,128)S(1)} %add.188), channel_id=1, source_target_pairs={{0,4},{4,0},{8,12},{12,8},{16,20},{20,16},{24,28},{28,24},{32,36},... | collective-permute-start | bytes 98312 | tf_op jit(solution)/shard_map/ppermute | solution.py:30
  74.0 4.0 %collective-permute-start.5 = (f32[128,64]{0,1:T(8,128)S(1)}, f32[128,64]{0,1:T(8,128)S(1)}, u32[]{:S(2)}, u32[]{:S(2)}) collective-permute-start(f32[128,64]{0,1:T(8,128)S(1)} %convolution_add_fusion.8), channel_id=1, source_target_pairs={{0,8},{4,12},{8,0},{12,4},{16,24},{20,28},{24,16},{28,20},{32,40},... | collective-permute-start | bytes 98312 | tf_op jit(solution)/shard_map/ppermute | solution.py:30
  78.2 4.9 %collective-permute-start.6 = (f32[128,64]{0,1:T(8,128)S(1)}, f32[128,64]{0,1:T(8,128)S(1)}, u32[]{:S(2)}, u32[]{:S(2)}) collective-permute-start(f32[128,64]{0,1:T(8,128)S(1)} %convolution_add_fusion.7), channel_id=1, source_target_pairs={{0,16},{4,20},{8,24},{12,28},{16,0},{20,4},{24,8},{28,12},{32,48},... | collective-permute-start | bytes 98312 | tf_op jit(solution)/shard_map/ppermute | solution.py:30
  83.3 7.9 %collective-permute-start.7 = (f32[128,64]{0,1:T(8,128)S(1)}, f32[128,64]{0,1:T(8,128)S(1)}, u32[]{:S(2)}, u32[]{:S(2)}) collective-permute-start(f32[128,64]{0,1:T(8,128)S(1)} %convolution_add_fusion.6), channel_id=1, source_target_pairs={{0,32},{4,36},{8,40},{12,44},{16,48},{20,52},{24,56},{28,60},{32,0... | collective-permute-start | bytes 98312 | tf_op jit(solution)/shard_map/ppermute | solution.py:30
  91.5 4.0 %collective-permute-start.8 = (f32[128,64]{0,1:T(8,128)S(1)}, f32[128,64]{0,1:T(8,128)S(1)}, u32[]{:S(2)}, u32[]{:S(2)}) collective-permute-start(f32[128,64]{0,1:T(8,128)S(1)} %convolution_add_fusion.5), channel_id=1, source_target_pairs={{0,64},{4,68},{8,72},{12,76},{16,80},{20,84},{24,88},{28,92},{32,9... | collective-permute-start | bytes 98312 | tf_op jit(solution)/shard_map/ppermute | solution.py:30
  95.7 7.7 %collective-permute-start.9 = (f32[128,64]{1,0:T(8,128)S(1)}, f32[128,64]{1,0:T(8,128)S(1)}, u32[]{:S(2)}, u32[]{:S(2)}) collective-permute-start(f32[128,64]{1,0:T(8,128)S(1)} %convolution_add_fusion), channel_id=1, source_target_pairs={{0,128},{4,132},{8,136},{12,140},{16,144},{20,148},{24,152},{28,15... | collective-permute-start | bytes 98312 | tf_op jit(solution)/shard_map/ppermute | solution.py:30
  103.4 2.9 %copy-start.4 = (f32[32,128,128]{1,2,0:T(8,128)S(1)}, f32[32,128,128]{1,2,0:T(8,128)}, u32[]{:S(2)}) copy-start(f32[32,128,128]{1,2,0:T(8,128)} %fusion.5) | copy-start | bytes 6291460
  103.6 2.8 %copy-start.3 = (f32[32,128,128]{1,2,0:T(8,128)S(1)}, f32[32,128,128]{1,2,0:T(8,128)}, u32[]{:S(2)}) copy-start(f32[32,128,128]{1,2,0:T(8,128)} %fusion.3) | copy-start | bytes 6291460
